TPU v7x, 256 devices: a whole 4x4x8 slice. The times are simulated.
256 devices in a mesh: seq: 8 (over y, core), frame: 32 (over x, z).
Axes of the slice: x: 4, y: 4, z: 8, core: 2. Of those that a mesh axis runs over, the one named last changes fastest.
Arguments:
- queries: bfloat16 [32, 2048, 128], P('frame', 'seq'), may hold values from -8 to 8
- out_grad: bfloat16 [32, 2048, 128], P('frame', 'seq'), may hold values from -6 to 6
- keys: bfloat16 [4096, 32, 128], P('frame', 'seq'), may hold values from -8 to 8
- values: bfloat16 [4096, 32, 128], P('frame', 'seq'), may hold values from -6 to 6
- limits: int32 [2048], P('seq'), may hold values from 1 to 4096, as said below
- block_start: int32 [32], P('frame'), may hold values from 0 to 3968, as said below
Outputs:
- query_grad: float32 [32, 2048, 128], P('frame', 'seq')
- key_grad: float32 [4096, 32, 128], P('frame', 'seq')
- value_grad: float32 [4096, 32, 128], P('frame', 'seq')
Inputs may be any that keep to these rules, and one draw needn't show every extreme that they name: `limits`: the last text row's limit is 4096. `block_start`: the entries are 128 times the block numbers 0 to 32 - 1, each once, in some order.
All inputs are finite; a program needn't handle non-finite values.
Results may differ from a plain program's by a relative error of at most 0.004.
The roundings to bfloat16 on the way count: a program that leaves them out, or rounds other values in their place, can miss the bound.
Values may be sent and summed in bfloat16 or wider, within the bound.
A program may use at most 64 MiB of HBM per device.

v0:
```python
import jax
import jax.numpy as jnp
from jax import lax
from jax.sharding import PartitionSpec as P

NEG = -1e30


def merged(shard, axis, combine):
    everything = jax.tree.map(lambda part: lax.all_gather(part, axis), shard)
    first = jax.tree.map(lambda part: part[0], everything)

    def turn(k, so_far):
        return combine(so_far, jax.tree.map(lambda part: part[k], everything))

    return lax.fori_loop(1, lax.axis_size(axis), turn, first)


def combine(first, second):
    top = jnp.maximum(first[0], second[0])
    return (top, first[1] * jnp.exp(first[0] - top) + second[1] * jnp.exp(second[0] - top))


def body(queries, out_grad, keys, values, limits, block_start):
    q_all, g_all = (
        lax.all_gather(queries, "frame", axis=0, tiled=True),
        lax.all_gather(out_grad, "frame", axis=0, tiled=True),
    )
    k_all, v_all = (
        lax.all_gather(keys, "seq", axis=1, tiled=True),
        lax.all_gather(values, "seq", axis=1, tiled=True),
    )
    heads, rows, width = q_all.shape
    frames = k_all.shape[0]
    factor = width ** (-0.5)
    stamp = block_start[0] + jnp.arange(frames, dtype=jnp.int32)
    visible = stamp[None, :] < limits[:, None]
    span = min(rows, 128)
    blocks = rows // span
    group = min(heads, 4)
    starts = jnp.arange(heads // group, dtype=jnp.int32) * group

    def scores_of(head_start, count, first_row):
        q_part = lax.dynamic_slice_in_dim(q_all, head_start, count, 0)[
            :, first_row : first_row + span
        ]
        k_part = lax.dynamic_slice_in_dim(k_all, head_start, count, 1)
        raw = (
            jnp.einsum("hrd,fhd->hrf", q_part, k_part, preferred_element_type=jnp.float32) * factor
        )
        mask = visible[first_row : first_row + span][None]
        return (jnp.where(mask, raw, NEG), q_part, k_part, mask)

    def dprobs_of(head_start, count, first_row):
        g_part = lax.dynamic_slice_in_dim(g_all, head_start, count, 0)[
            :, first_row : first_row + span
        ]
        v_part = lax.dynamic_slice_in_dim(v_all, head_start, count, 1)
        return (
            jnp.einsum("hrd,fhd->hrf", g_part, v_part, preferred_element_type=jnp.float32),
            g_part,
        )

    def stats_block(first_row):

        def stats_one_group(head_start):
            scores, _, _, mask = scores_of(head_start, group, first_row)
            top_here = jnp.max(scores, axis=-1)
            expo = jnp.where(mask, jnp.exp(scores - top_here[..., None]), jnp.float32(0.0))
            return (top_here, jnp.sum(expo, axis=-1))

        top_here, total_here = lax.map(stats_one_group, starts)
        return (top_here.reshape(heads, span), total_here.reshape(heads, span))

    pieces = [stats_block(index * span) for index in range(blocks)]
    local_top = jnp.concatenate([piece[0] for piece in pieces], axis=1)
    local_total = jnp.concatenate([piece[1] for piece in pieces], axis=1)
    top, total = merged((local_top, local_total), "frame", combine)

    def dots_block(first_row):

        def dots_one_group(head_start):
            scores, _, _, mask = scores_of(head_start, group, first_row)
            top_part = lax.dynamic_slice_in_dim(top, head_start, group, 0)[
                :, first_row : first_row + span
            ]
            total_part = lax.dynamic_slice_in_dim(total, head_start, group, 0)[
                :, first_row : first_row + span
            ]
            expo = jnp.where(mask, jnp.exp(scores - top_part[..., None]), jnp.float32(0.0))
            probs = expo / total_part[..., None]
            dprobs, _ = dprobs_of(head_start, group, first_row)
            return jnp.sum(probs * dprobs, axis=-1)

        return lax.map(dots_one_group, starts).reshape(heads, span)

    local_delta = jnp.concatenate([dots_block(index * span) for index in range(blocks)], axis=1)
    delta = lax.psum(local_delta, "frame")

    def probs_of(scores, mask, head_start, count, first_row):
        top_part = lax.dynamic_slice_in_dim(top, head_start, count, 0)[
            :, first_row : first_row + span
        ]
        total_part = lax.dynamic_slice_in_dim(total, head_start, count, 0)[
            :, first_row : first_row + span
        ]
        expo = jnp.where(mask, jnp.exp(scores - top_part[..., None]), jnp.float32(0.0))
        return expo / total_part[..., None]

    def grads_of(head_start, count, first_row):
        scores, q_part, k_part, mask = scores_of(head_start, count, first_row)
        probs = probs_of(scores, mask, head_start, count, first_row)
        dprobs, g_part = dprobs_of(head_start, count, first_row)
        delta_part = lax.dynamic_slice_in_dim(delta, head_start, count, 0)[
            :, first_row : first_row + span
        ]
        dscores = (probs * (dprobs - delta_part[..., None])).astype(jnp.bfloat16)
        probs_low = probs.astype(jnp.bfloat16)
        dq = (
            jnp.einsum("hrf,fhd->hrd", dscores, k_part, preferred_element_type=jnp.float32) * factor
        )
        dk = (
            jnp.einsum("hrf,hrd->fhd", dscores, q_part, preferred_element_type=jnp.float32) * factor
        )
        dv = jnp.einsum("hrf,hrd->fhd", probs_low, g_part, preferred_element_type=jnp.float32)
        return (dq, dk, dv)

    def accumulate(carry, first_row):

        def step(state, head_start):
            dq, dk, dv = grads_of(head_start, group, first_row)
            key_acc = lax.dynamic_update_slice_in_dim(
                state[0],
                lax.dynamic_slice_in_dim(state[0], head_start, group, 1) + dk,
                head_start,
                1,
            )
            value_acc = lax.dynamic_update_slice_in_dim(
                state[1],
                lax.dynamic_slice_in_dim(state[1], head_start, group, 1) + dv,
                head_start,
                1,
            )
            return ((key_acc, value_acc), dq)

        state, dq_groups = lax.scan(step, carry, starts)
        return (state, dq_groups.reshape(heads, span, width))

    zeros_kv = jnp.zeros((frames, heads, width), jnp.float32)
    state = (zeros_kv, zeros_kv)
    dq_blocks = []
    for index in range(blocks):
        state, dq_block = accumulate(state, index * span)
        dq_blocks.append(dq_block)
    key_terms, value_terms = state
    dq_terms = jnp.concatenate(dq_blocks, axis=1)
    query_grad = lax.psum_scatter(dq_terms, "frame", scatter_dimension=0, tiled=True)
    key_grad, value_grad = (
        lax.psum_scatter(key_terms, "seq", scatter_dimension=1, tiled=True),
        lax.psum_scatter(value_terms, "seq", scatter_dimension=1, tiled=True),
    )
    return (query_grad, key_grad, value_grad)


def solution(mesh):
    placed = (
        P("frame", "seq", None),
        P("frame", "seq", None),
        P("frame", "seq", None),
        P("frame", "seq", None),
        P("seq"),
        P("frame"),
    )
    return jax.shard_map(
        body,
        mesh=mesh,
        in_specs=placed,
        out_specs=(P("frame", "seq", None), P("frame", "seq", None), P("frame", "seq", None)),
        check_vma=False,
    )
```

profile of v0, /device:TPU:4, one launch (start us, length us, event | category | flops | bytes accessed | tf_op | source)
XLA Modules:
  0.0 1109.6 jit_solution(6087999004672252762)
XLA Ops:
  7.2 1.6 copy.25
  11.2 28.1 %all-gather.11.cloned.1.call-done = bf16[128,32,128]{2,0,1:T(8,128)(2,1)} async-done(((bf16[128,4,128]{2,0,1:T(8,128)(2,1)}), bf16[128,32,128]{2,0,1:T(8,128)(2,1)}) %all-gather.11.cloned.1.call-update) | async-done | bytes 1048592 | tf_op jit(solution)/shard_map/all_gather | solution.py:30
  39.3 79.1 %all-gather.9.cloned.1.call-done = bf16[32,256,128]{2,1,0:T(8,128)(2,1)} async-done(((bf16[1,256,128]{2,1,0:T(8,128)(2,1)}), bf16[32,256,128]{2,1,0:T(8,128)(2,1)}) %all-gather.9.cloned.1.call-update) | async-done | bytes 2097168 | tf_op jit(solution)/shard_map/all_gather | solution.py:26
  118.4 30.8 %while.89 = (s32[]{:T(128)}, f32[8,4,128]{2,1,0:T(4,128)S(1)}, f32[8,4,128]{2,1,0:T(4,128)S(1)}, pred[256,128]{0,1:T(8,128)(4,1)S(1)}, s32[8]{0:T(128)S(1)}, /*i...) while((s32[]{:T(128)}, f32[8,4,128]{2,1,0:T(4,128)S(1)}, ...), condition=%wide.region_3.4_spmd, body=%wide.region_0.3_spmd.sunk | while | flops 17169412 | bytes 867479 | solution.py:72
  132.5 1.2 fusion.139
  136.4 1.2 fusion.139
  140.2 1.2 fusion.139
  149.3 30.9 %while.90 = (s32[]{:T(128)}, f32[8,4,128]{2,1,0:T(4,128)S(1)}, f32[8,4,128]{2,1,0:T(4,128)S(1)}, pred[256,128]{0,1:T(8,128)(4,1)S(1)}, s32[8]{0:T(128)S(1)}, /*i...) while((s32[]{:T(128)}, f32[8,4,128]{2,1,0:T(4,128)S(1)}, ...), condition=%wide.region_7.8_spmd, body=%wide.region_4.7_spmd.sunk | while | flops 17169412 | bytes 868011 | solution.py:72
  151.8 1.2 fusion.140
  155.7 1.2 fusion.140
  159.6 1.2 fusion.140
  163.4 1.2 fusion.140
  167.3 1.2 fusion.140
  171.1 1.2 fusion.140
  175.0 1.2 fusion.140
  178.8 1.2 fusion.140
  182.9 71.8 %all-gather.17.cloned.1.call-done = f32[1024,256]{1,0:T(8,128)} async-done(((f32[32,256]{1,0:T(8,128)}), f32[1024,256]{1,0:T(8,128)}) %all-gather.17.cloned.1.call-update) | async-done | bytes 1048592 | tf_op jit(solution)/shard_map/all_gather | solution.py:10
  255.4 76.1 %all-gather.19.cloned.1.call-done = f32[1024,256]{1,0:T(8,128)} async-done(((f32[32,256]{1,0:T(8,128)}), f32[1024,256]{1,0:T(8,128)}) %all-gather.19.cloned.1.call-update) | async-done | bytes 1048592 | tf_op jit(solution)/shard_map/all_gather | solution.py:10
  332.2 25.9 %while.91 = (s32[]{:T(128)}, f32[32,256]{1,0:T(8,128)S(1)}, f32[32,256]{1,0:T(8,128)S(1)}, f32[32,32,256]{2,1,0:T(8,128)}, f32[32,32,256]{2,1,0:T(8,128)}, /*index=5*/s32[]{:T(128)}, s32[]{:T(128)}, s32[]{:T(128)}) while((s32[]{:T(128)}, f32[32,256]{1,0:T(8,128)S(1)}, f32[32,256]{1,0:T(8,128)S(1)}, f32[32,32,256]{2,1,0:T(8,128)}, ...), condition=%wide.region_9.10_spmd, body=%wide.region_8.9_spmd.sunk | while | flops 49157 | bytes 196739 | solution.py:16
  358.3 78.9 %all-gather.13.cloned.1.call-done = bf16[32,256,128]{2,1,0:T(8,128)(2,1)} async-done(((bf16[1,256,128]{2,1,0:T(8,128)(2,1)}), bf16[32,256,128]{2,1,0:T(8,128)(2,1)}) %all-gather.13.cloned.1.call-update) | async-done | bytes 2097168 | tf_op jit(solution)/shard_map/all_gather | solution.py:27
  437.3 40.1 %while.92 = (s32[]{:T(128)}, f32[8,4,128]{2,1,0:T(4,128)S(1)}, pred[256,128]{0,1:T(8,128)(4,1)S(1)}, s32[8]{0:T(128)S(1)}, bf16[32,256,128]{2,1,0:T(8,128)(2,1)}...) while((s32[]{:T(128)}, f32[8,4,128]{2,1,0:T(4,128)S(1)}, ...), condition=%wide.region_12.13_spmd, body=%wide.region_10.12_spmd.sunk | while | flops 34012676 | bytes 1118387 | solution.py:95
  439.8 1.2 fusion.146
  444.8 1.2 fusion.146
  449.9 1.2 fusion.146
  454.9 1.2 fusion.146
  456.1 1.2 fusion.147
  459.9 1.2 fusion.146
  464.9 1.2 fusion.146
  469.9 1.2 fusion.146
  471.1 1.2 fusion.147
  474.9 1.2 fusion.146
  477.4 41.1 %while.93 = (s32[]{:T(128)}, f32[8,4,128]{2,1,0:T(4,128)S(1)}, pred[256,128]{0,1:T(8,128)(4,1)S(1)}, s32[8]{0:T(128)S(1)}, bf16[32,256,128]{2,1,0:T(8,128)(2,1)}...) while((s32[]{:T(128)}, f32[8,4,128]{2,1,0:T(4,128)S(1)}, ...), condition=%wide.region_15.16_spmd, body=%wide.region_13.15_spmd.sunk | while | flops 34012676 | bytes 1119435 | solution.py:95
  517.3 1.2 fusion.153
  518.5 120.4 %psum.7 = f32[32,256]{1,0:T(8,128)S(1)} all-reduce(f32[32,256]{1,0:T(8,128)S(1)} %pad_maximum_fusion.3), channel_id=1, replica_groups=mesh['seq'=8,'frame'=32] {'frame'}, use_global_device_ids=true, to_apply=%region_16.17 | all-reduce | flops 8192 | bytes 65536 | tf_op jit(solution)/shard_map/psum | solution.py:98
  638.9 1.6 broadcast.56.clone
  640.7 1.6 broadcast_in_dim.141.clone
  642.4 71.8 %while.94 = (s32[]{:T(128)}, f32[128,32,128]{0,2,1:T(8,128)S(1)}, f32[128,32,128]{0,2,1:T(8,128)}, f32[8,4,128,128]{3,2,1,0:T(8,128)}, s32[8]{0:T(128)S(1)}, /*i...) while((s32[]{:T(128)}, f32[128,32,128]{0,2,1:T(8,128)S(1)}, ...), condition=%wide.region_18.19_spmd, body=%wide.region_17.18_spmd.sunk | while | flops 84738048 | bytes 3480271 | solution.py:146
  649.4 2.0 fusion.167
  658.3 2.0 fusion.167
  667.3 2.0 fusion.167
  676.3 2.0 fusion.167
  685.2 2.0 fusion.167
  694.2 2.0 fusion.167
  703.2 2.0 fusion.167
  712.2 2.0 fusion.167
  714.1 1.6 broadcast.56
  715.7 73.1 %while.95 = (s32[]{:T(128)}, f32[128,32,128]{0,2,1:T(8,128)S(1)}, f32[128,32,128]{0,2,1:T(8,128)}, f32[8,4,128,128]{3,2,1,0:T(8,128)}, s32[8]{0:T(128)S(1)}, /*i...) while((s32[]{:T(128)}, f32[128,32,128]{0,2,1:T(8,128)S(1)}, ...), condition=%wide.region_20.21_spmd, body=%wide.region_19.20_spmd.sunk | while | flops 84738048 | bytes 3482343 | solution.py:146
  722.9 2.0 fusion.182
  732.0 2.0 fusion.182
  741.1 2.0 fusion.182
  750.3 2.0 fusion.182
  759.4 2.0 fusion.182
  768.6 2.0 fusion.182
  777.7 2.0 fusion.182
  786.9 2.0 fusion.182
  788.8 1.8 copy.31
  790.7 2.9 copy.32
  793.7 1.5 copy-done
  795.2 4.0 pad_maximum_fusion
  799.3 42.5 %reduce-scatter.6.cloned.1.call-done = f32[128,4,128]{2,0,1:T(8,128)} async-done(((f32[128,32,128]{2,0,1:T(8,128)}), f32[128,4,128]{2,0,1:T(8,128)}) %reduce-scatter.6.cloned.1.call-update) | async-done | bytes 262160 | tf_op jit(solution)/shard_map/reduce_scatter | solution.py:159
  841.8 1.8 copy.33
  843.6 35.8 %reduce-scatter.8.cloned.1.call-done = f32[128,4,128]{2,0,1:T(8,128)} async-done(((f32[128,32,128]{2,0,1:T(8,128)}), f32[128,4,128]{2,0,1:T(8,128)}) %reduce-scatter.8.cloned.1.call-update) | async-done | bytes 262160 | tf_op jit(solution)/shard_map/reduce_scatter | solution.py:160
  879.5 1.8 copy.34
  881.3 221.7 %reduce-scatter.4.cloned.1.call-done = f32[1,256,128]{2,1,0:T(8,128)} async-done(((f32[32,256,128]{2,1,0:T(8,128)}), f32[1,256,128]{2,1,0:T(8,128)}) %reduce-scatter.4.cloned.1.call-update) | async-done | bytes 131088 | tf_op jit(solution)/shard_map/reduce_scatter | solution.py:157
  (370 shorter events, 166.3 us)
Async XLA Ops:
  7.2 32.2 %all-gather.11.cloned.1.call-start = ((), (), s32[]{:S(2)}) async-start(), calls=%async_computation.4 | async-start | bytes 1179648 | tf_op jit(solution)/shard_map/all_gather | solution.py:30
  8.8 109.6 %all-gather.9.cloned.1.call-start = ((), (), s32[]{:S(2)}) async-start(), calls=%async_computation.3 | async-start | bytes 2162688 | tf_op jit(solution)/shard_map/all_gather | solution.py:26
  9.6 245.1 %all-gather.17.cloned.1.call-start = ((), (), s32[]{:S(2)}) async-start(), calls=%async_computation.10 | async-start | bytes 1081344 | tf_op jit(solution)/shard_map/all_gather | solution.py:10
  149.3 32.3 %copy-start.2 = (bf16[128,4,128]{2,1,0:T(4,128)(2,1)S(1)}, bf16[128,4,128]{2,1,0:T(4,128)(2,1)}, u32[]{:S(2)}) copy-start(bf16[128,4,128]{2,1,0:T(4,128)(2,1)} %param.23) | copy-start | bytes 393220
  180.8 150.7 %all-gather.19.cloned.1.call-start = ((), (), s32[]{:S(2)}) async-start(), calls=%async_computation.11 | async-start | bytes 1081344 | tf_op jit(solution)/shard_map/all_gather | solution.py:10
  181.5 176.8 %all-gather.15.cloned.1.call-start = ((), (), s32[]{:S(2)}) async-start(), calls=%async_computation.6 | async-start | bytes 1179648 | tf_op jit(solution)/shard_map/all_gather | solution.py:31
  182.2 255.0 %all-gather.13.cloned.1.call-start = ((), (), s32[]{:S(2)}) async-start(), calls=%async_computation.5 | async-start | bytes 2162688 | tf_op jit(solution)/shard_map/all_gather | solution.py:27
  182.8 659.0 %reduce-scatter.6.cloned.1.call-start = ((), (), s32[]{:S(2)}) async-start(), calls=%async_computation.8 | async-start | bytes 2359296 | tf_op jit(solution)/shard_map/reduce_scatter | solution.py:159
  640.5 1.9 copy-start.1
  790.7 88.8 %reduce-scatter.8.cloned.1.call-start = ((), (), s32[]{:S(2)}) async-start(), calls=%async_computation.9 | async-start | bytes 2359296 | tf_op jit(solution)/shard_map/reduce_scatter | solution.py:160
  793.6 1.6 copy-start
  793.7 309.4 %reduce-scatter.4.cloned.1.call-start = ((), (), s32[]{:S(2)}) async-start(), calls=%async_computation.7 | async-start | bytes 4325376 | tf_op jit(solution)/shard_map/reduce_scatter | solution.py:157
Sparse Core Ops, SparseCore 0:
  10.4 28.8 all-gather.10
  41.9 76.4 all-gather.8
  180.9 73.7 all-gather.16
  257.7 73.7 all-gather.18
  333.8 24.5 all-gather.14
  360.8 76.4 all-gather.12
  790.8 50.9 reduce-scatter.5
  844.4 35.0 reduce-scatter.7
  883.9 219.0 reduce-scatter.3
where the time goes:
time: 1120 us; the launch traced here: 1110 us
  waiting for transfers between devices  636 us (57%)
  matrix products  159 us (14%)
  blocking collectives  120 us (11%)
  loops' own time  95.6 us (9%)
  local copies, waits for them, and re-layouts  51.1 us (5%)
  other arithmetic  32.4 us (3%)
  between operations  14.6 us (1%)
    reduce_scatter x1, waiting for transfers between devices, body(): lax.psum_scatter(dq_terms, 'frame', scatter_dimension=0, tiled=True)  222 us
    all_gather x2, waiting for transfers between devices, merged(): everything = jax.tree.map(lambda part: lax.all_gather(part, axis), shard)  148 us
    psum x1, blocking collectives, body(): delta = lax.psum(local_delta, 'frame')  120 us
    all_gather x1, waiting for transfers between devices, body(): lax.all_gather(queries, 'frame', axis=0, tiled=True)  79.1 us
    all_gather x1, waiting for transfers between devices, body(): lax.all_gather(out_grad, 'frame', axis=0, tiled=True)  78.9 us
    dot_general x48, matrix products, scores_of(): jnp.einsum('hrd,fhd->hrf', q_part, k_part, preferred_element_type=jnp.flo...  57 us
    reduce_scatter x1, waiting for transfers between devices, body(): lax.psum_scatter(key_terms, 'seq', scatter_dimension=1, tiled=True)  42.5 us
    dot_general x32, matrix products, dprobs_of(): jnp.einsum('hrd,fhd->hrf', g_part, v_part, preferred_element_type=jnp.flo...  38.1 us
  transfers between devices with their start and end apart: 9, of which 9 were waited for; matrix products, arithmetic and copies ran while one was open for 4% of the time, Pallas kernels for 0%

commit v1 on v0

v1 whole, which is shorter than its diff:
```python
import functools

import jax
import jax.numpy as jnp
from jax import lax
from jax.experimental import pallas as pl
from jax.experimental.pallas import tpu as pltpu
from jax.sharding import PartitionSpec as P

MESH = pl.DeviceIdType.MESH
NEG = -1e30
FLOOR = -1e29
NT = (((1,), (1,)), ((), ()))


def kernel(
    nx, ny, nz,
    q_hbm, g_hbm, k_hbm, v_hbm, lim_hbm, bs_ref,
    out_in, dq_in,
    q_ref, g_ref, k_ref, v_ref, lim_ref,
    stage, kv_all, kt, q_all, g_all, lim_all, s_buf, dp_buf, m_blk, l_blk, d_blk, stat_all,
    part, part_in, out_send, dq_send, relay,
    in_ss, kv_ss, kv_rs, fw_ss, qg_ss, qg_rs, st_ss, st_rs, pt_ss, pt_rs, out_ss, out_rs,
    dy_ss, dy_rs, dx_ss, dx_rs,
):
    heads = nz // 2
    frames, _, width = k_ref.shape
    rows = q_ref.shape[0]
    factor = width ** (-0.5)
    seq, frame = lax.axis_index("seq"), lax.axis_index("frame")
    y, c = lax.div(seq, 2), lax.rem(seq, 2)
    x, z = lax.div(frame, nz), lax.rem(frame, nz)
    zc, zj, zp, zt = lax.div(z, heads), lax.rem(z, heads), lax.rem(z, 2), lax.div(z, 2)

    def at(px, py, pz, pc):
        return (py * 2 + pc, px * nz + pz)

    def near(k):
        if isinstance(k, int):
            step = (k + 1) // 2 if k % 2 else ny - k // 2
        else:
            step = jnp.where(lax.rem(k, 2) == 1, lax.div(k + 1, 2), ny - lax.div(k, 2))
        return lax.rem(y + step, ny)

    own_kv = jnp.logical_and(zc == c, zp == c)
    partner = at(x, y, z, 1 - c)
    kv_to = [at(x, y, heads * c + j, zp) for j in range(heads)]
    kv_from = [at(x, y, 2 * t + c, zc) for t in range(heads)]
    qg_to = [at(i, x, z, c) for i in range(nx)]
    qg_from = [at(y, i, z, c) for i in range(ny)]
    x_line = [at(i, y, z, c) for i in range(nx)]
    y_line = [at(x, i, z, c) for i in range(ny)]
    kv_to_self = [jnp.logical_and(own_kv, zj == j) for j in range(heads)]
    kv_from_self = [jnp.logical_and(own_kv, zt == t) for t in range(heads)]
    qg_to_self = [jnp.logical_and(x == y, x == i) for i in range(nx)]
    qg_from_self = [jnp.logical_and(x == y, y == i) for i in range(ny)]
    x_self = [x == i for i in range(nx)]
    y_self = [y == i for i in range(ny)]

    def remote(src, dst, ss, rs, to):
        return pltpu.make_async_remote_copy(
            src_ref=src, dst_ref=dst, send_sem=ss, recv_sem=rs, device_id=to, device_id_type=MESH
        )

    def send(src, dst, ss, rs, to, is_self):
        @pl.when(is_self)
        def _():
            pltpu.make_async_copy(src, dst, rs).start()

        @pl.when(jnp.logical_not(is_self))
        def _():
            remote(src, dst, ss, rs, to).start()

    def sent(src, dst, ss, rs, to, is_self):
        @pl.when(jnp.logical_not(is_self))
        def _():
            remote(src, dst, ss, rs, to).wait_send()

    def arrived(dst, rs):
        pltpu.make_async_copy(dst, dst, rs).wait()

    barrier = pltpu.get_barrier_semaphore()
    pl.semaphore_signal(barrier, inc=1, device_id=partner, device_id_type=MESH)
    count = jnp.int32(1)
    for to, is_self in zip(
        kv_from + kv_to + qg_from + qg_to + x_line + y_line,
        kv_from_self + kv_to_self + qg_from_self + qg_to_self + x_self + y_self,
    ):
        @pl.when(jnp.logical_not(is_self))
        def _(to=to):
            pl.semaphore_signal(barrier, inc=1, device_id=to, device_id_type=MESH)

        count = count + jnp.where(is_self, 0, 1)

    fetches = [
        pltpu.make_async_copy(src, dst, in_ss.at[n])
        for n, (src, dst) in enumerate(
            [(k_hbm, k_ref), (v_hbm, v_ref), (q_hbm, q_ref), (g_hbm, g_ref), (lim_hbm, lim_ref)]
        )
    ]
    for fetch in fetches:
        fetch.start()
    start_rows = jnp.full((16, width), bs_ref[0], jnp.int32).astype(jnp.float32)
    for j in range(heads):
        stage[j, 2 * frames :] = start_rows.astype(jnp.bfloat16)
    part[...] = jnp.zeros_like(part)
    fetches[0].wait()
    for j in range(heads):
        stage[j, 0:frames] = k_ref[:, j, :]
    fetches[1].wait()
    for j in range(heads):
        stage[j, frames : 2 * frames] = v_ref[:, j, :]
    for fetch in fetches[2:]:
        fetch.wait()

    pl.semaphore_wait(barrier, count)

    def kv_msg(j):
        return (stage.at[j], kv_all.at[z], kv_ss.at[j], kv_rs.at[z], kv_to[j], kv_to_self[j])

    def qg_msgs(i):
        return [
            (src, dst.at[y], qg_ss.at[n, i], qg_rs.at[n, y], qg_to[i], qg_to_self[i])
            for n, (src, dst) in enumerate([(q_ref, q_all), (g_ref, g_all), (lim_ref, lim_all)])
        ]

    def send_kv(n, _):
        j = lax.rem(zj + jnp.where(zc == c, heads - 1 - n + lax.div(heads, 2), n), heads)
        is_self = jnp.logical_and(own_kv, zj == j)
        send(
            stage.at[j], kv_all.at[z], kv_ss.at[j], kv_rs.at[z], at(x, y, heads * c + j, zp), is_self
        )
        return 0

    for i in range(nx):
        for msg in qg_msgs(i)[:2]:
            send(*msg)
    lax.fori_loop(0, heads, send_kv, 0)
    for i in range(nx):
        send(*qg_msgs(i)[2])

    place = lax.broadcasted_iota(jnp.int32, (frames, rows), 0).astype(jnp.float32)

    def block(b, i):
        here = pl.ds(pl.multiple_of(b * frames, frames), frames)
        k = kv_all[b, 0:frames]
        v = kv_all[b, frames : 2 * frames]
        start = kv_all[b, 2 * frames :].astype(jnp.float32)[0:1, :]
        limit = lim_all[i].astype(jnp.float32)
        room = jnp.concatenate(
            [limit[n : n + 1, :] - start[:, 0 : limit.shape[1]] for n in range(limit.shape[0])],
            axis=1,
        )
        raw = lax.dot_general(k, q_all[i], NT, preferred_element_type=jnp.float32)
        s = jnp.where(place < room, raw * factor, NEG)
        top = jnp.maximum(jnp.max(s, axis=0, keepdims=True), FLOOR)
        e = jnp.exp(s - top)
        dp = lax.dot_general(v, g_all[i], NT, preferred_element_type=jnp.float32)
        s_buf[i, here] = s
        dp_buf[i, here] = dp
        m_blk[i, pl.ds(b, 1)] = top
        l_blk[i, pl.ds(b, 1)] = jnp.sum(e, axis=0, keepdims=True)
        d_blk[i, pl.ds(b, 1)] = jnp.sum(e * dp, axis=0, keepdims=True)

    def st_msg(i, n):
        return (
            stat_all.at[x, i], stat_all.at[x, i], st_ss.at[n, i], st_rs.at[x, i], x_line[n],
        )

    def share_stats(i):
        m_all = m_blk[i]
        m = jnp.max(m_all, axis=0, keepdims=True)
        w = jnp.exp(m_all - m)
        stat_all[x, i, 0:1] = m
        stat_all[x, i, 1:2] = jnp.sum(w * l_blk[i], axis=0, keepdims=True)
        stat_all[x, i, 2:3] = jnp.sum(w * d_blk[i], axis=0, keepdims=True)
        stat_all[x, i, 3:4] = jnp.zeros_like(m)
        for n in range(nx):
            @pl.when(jnp.logical_not(x_self[n]))
            def _(n=n):
                remote(*st_msg(i, n)).start()

    def text_arrived(i):
        arrived(q_all.at[i], qg_rs.at[0, i])
        arrived(g_all.at[i], qg_rs.at[1, i])
        arrived(lim_all.at[i], qg_rs.at[2, i])

    base = z + lax.rem(z + c, 2)
    other = z + lax.rem(z + 1 - c, 2)

    def pair(n):
        m = lax.div(n + 1, 2) * 2
        step = jnp.where(lax.rem(n, 2) == 1, nz - m, m)
        return lax.rem(base + step, nz), lax.rem(other + step, nz)

    def take(b):
        arrived(kv_all.at[b], kv_rs.at[b])
        remote(kv_all.at[b], kv_all.at[b], fw_ss.at[b], kv_rs.at[b], partner).start()
        kt[b] = kv_all[b, 0:frames].T

    def take_passed(b):
        arrived(kv_all.at[b], kv_rs.at[b])
        kt[b] = kv_all[b, 0:frames].T

    def first_step(n, _):
        b, b2 = pair(n)
        take(b)
        block(b, y)
        take_passed(b2)
        block(b2, y)
        return 0

    def step(i, n, _):
        b, b2 = pair(n)
        block(b, i)
        block(b2, i)
        return 0

    def near_blocks(i):
        text_arrived(i)
        lax.fori_loop(0, heads - 1, functools.partial(step, i), 0)

    def far_blocks(k, _):
        i = near(k)
        step(i, jnp.int32(heads - 1), 0)
        share_stats(i)
        return 0

    text_arrived(y)
    lax.fori_loop(0, heads - 1, first_step, 0)
    near_blocks(near(1))
    last, last2 = pair(jnp.int32(heads - 1))
    take(last)
    if ny > 3:
        near_blocks(near(2))
    take_passed(last2)
    lax.fori_loop(0, max(ny - 1, 2), far_blocks, 0)
    if ny > 2:
        text_arrived(near(ny - 1))
        lax.fori_loop(0, heads, functools.partial(step, near(ny - 1)), 0)
        share_stats(near(ny - 1))

    def part_msg(t):
        return (part.at[t, 1 - c], part_in.at[t], pt_ss.at[t], pt_rs.at[t], partner)

    def out_msg(t):
        return (
            out_send.at[t], out_in.at[zj], out_ss.at[t], out_rs.at[zj],
            at(x, y, 2 * t + c, zc), jnp.logical_and(own_kv, zt == t),
        )

    def finish(t):
        arrived(part_in.at[t], pt_rs.at[t])
        out_send[t, 0] = ((part[t, c, 0] + part_in[t, 0]) * factor).astype(jnp.bfloat16)
        out_send[t, 1] = (part[t, c, 1] + part_in[t, 1]).astype(jnp.bfloat16)
        send(*out_msg(t))

    def dx_msg(a):
        return (relay.at[a], dq_in.at[x], dx_ss.at[a], dx_rs.at[x], at(a, y, z, c), x == a)

    def dy_msg(i):
        return (dq_send.at[i], relay.at[y], dy_ss.at[i], dy_rs.at[y], at(x, i, z, c))

    def far(t):
        return lax.rem(zt + [2, 1, 3, 0][t] if heads == 4 else zt + t, heads)

    def grads_chunk(i, last):
        for n in range(nx):
            @pl.when(jnp.logical_not(x_self[n]))
            def _(n=n):
                arrived(stat_all.at[n, i], st_rs.at[n, i])

        stats = [stat_all[n, i] for n in range(nx)]
        top = functools.reduce(jnp.maximum, [s[0:1] for s in stats])
        shares = [jnp.exp(s[0:1] - top) for s in stats]
        total = sum(w * s[1:2] for w, s in zip(shares, stats))
        delta = sum(w * s[2:3] for w, s in zip(shares, stats)) / total
        dqt = jnp.zeros((width, rows), jnp.float32)
        for n in range(heads):
            t = far(n)
            ds, low = [], []
            for h in range(2):
                b = 2 * t + h
                here = pl.ds(pl.multiple_of(b * frames, frames), frames)
                p = jnp.exp(s_buf[i, here] - top) / total
                ds.append((p * (dp_buf[i, here] - delta)).astype(jnp.bfloat16))
                low.append(p.astype(jnp.bfloat16))
            for h in range(2):
                part[t, h, 0] += jnp.dot(ds[h], q_all[i], preferred_element_type=jnp.float32)
                part[t, h, 1] += jnp.dot(low[h], g_all[i], preferred_element_type=jnp.float32)
            if last:
                remote(*part_msg(t)).start()
            dqt += jnp.dot(
                jnp.concatenate([kt[2 * t], kt[2 * t + 1]], axis=1),
                jnp.concatenate(ds, axis=0),
                preferred_element_type=jnp.float32,
            )
        return dqt.T * factor

    relay[y] = grads_chunk(y, False)
    send(*dx_msg(y))

    def middle(k, _):
        i = near(k)
        dq_send[i] = grads_chunk(i, False)
        remote(*dy_msg(i)).start()
        return 0

    lax.fori_loop(1, ny - 1, middle, 0)
    i = near(ny - 1)
    dq_send[i] = grads_chunk(i, True)
    remote(*dy_msg(i)).start()

    def pass_on(a):
        arrived(relay.at[a], dy_rs.at[a])
        send(*dx_msg(a))

    for n in range(heads):
        finish(far(n))
        if 1 <= n < ny - 1:
            pass_on(near(n))
    pass_on(near(ny - 1))

    for j in range(heads):
        arrived(out_in.at[j], out_rs.at[j])
    for i in range(nx):
        arrived(dq_in.at[i], dx_rs.at[i])

    for j in range(heads):
        sent(*kv_msg(j))
    for i in range(nx):
        for msg in qg_msgs(i):
            sent(*msg)

    def sent_step(n, _):
        b = pair(n)[0]
        remote(kv_all.at[b], kv_all.at[b], fw_ss.at[b], kv_rs.at[b], partner).wait_send()
        remote(*part_msg(n)).wait_send()
        sent(*out_msg(n))
        return 0

    def sent_chunk(i, _):
        for n in range(nx):
            @pl.when(jnp.logical_not(x_self[n]))
            def _(n=n):
                remote(*st_msg(i, n)).wait_send()

        @pl.when(i != y)
        def _():
            remote(*dy_msg(i)).wait_send()

        sent(*dx_msg(i))
        return 0

    lax.fori_loop(0, heads, sent_step, 0)
    lax.fori_loop(0, ny, sent_chunk, 0)


def place(out_in, dq_in, dq_hbm, dk_hbm, dv_hbm, dq, dk, dv, sems):
    dq[...] = functools.reduce(jnp.add, [dq_in[i] for i in range(dq_in.shape[0])])
    writes = [pltpu.make_async_copy(dq, dq_hbm, sems.at[0])]
    writes[0].start()
    for n, (buf, hbm) in enumerate([(dk, dk_hbm), (dv, dv_hbm)]):
        for j in range(out_in.shape[0]):
            buf[:, j, :] = out_in[j, n].astype(jnp.float32)
        writes.append(pltpu.make_async_copy(buf, hbm, sems.at[n + 1]))
        writes[-1].start()
    for write in writes:
        write.wait()


def body(nx, ny, nz, queries, out_grad, keys, values, limits, block_start):
    _, rows, width = queries.shape
    frames, heads, _ = keys.shape
    text, all_frames = ny * rows, nz * frames
    bf16, f32, dma, vmem = jnp.bfloat16, jnp.float32, pltpu.SemaphoreType.DMA, pltpu.VMEM
    lanes = min(rows, 128)
    limits = limits.reshape(rows // lanes, lanes)
    in_vmem = pl.BlockSpec(memory_space=pltpu.VMEM)
    in_hbm = pl.BlockSpec(memory_space=pltpu.HBM)
    out_in, dq_in = pl.pallas_call(
        functools.partial(kernel, nx, ny, nz),
        out_shape=(
            jax.ShapeDtypeStruct((heads, 2, frames, width), bf16),
            jax.ShapeDtypeStruct((nx, rows, width), f32),
        ),
        in_specs=[in_hbm] * 5 + [pl.BlockSpec(memory_space=pltpu.SMEM)],
        out_specs=[in_vmem] * 2,
        scratch_shapes=[
            vmem((rows, width), bf16),
            vmem((rows, width), bf16),
            vmem(keys.shape, bf16),
            vmem(keys.shape, bf16),
            vmem(limits.shape, jnp.int32),
            vmem((heads, 2 * frames + 16, width), bf16),
            vmem((nz, 2 * frames + 16, width), bf16),
            vmem((nz, width, frames), bf16),
            vmem((ny, rows, width), bf16),
            vmem((ny, rows, width), bf16),
            vmem((ny,) + limits.shape, jnp.int32),
            vmem((ny, all_frames, rows), f32),
            vmem((ny, all_frames, rows), f32),
            vmem((ny, nz, rows), f32),
            vmem((ny, nz, rows), f32),
            vmem((ny, nz, rows), f32),
            vmem((nx, ny, 4, rows), f32),
            vmem((heads, 2, 2, frames, width), f32),
            vmem((heads, 2, frames, width), f32),
            vmem((heads, 2, frames, width), bf16),
            vmem((ny, rows, width), f32),
            vmem((ny, rows, width), f32),
            dma((5,)),
            dma((heads,)), dma((nz,)), dma((nz,)),
            dma((3, nx)), dma((3, ny)),
            dma((nx, ny)), dma((nx, ny)),
            dma((heads,)), dma((heads,)),
            dma((heads,)), dma((heads,)),
            dma((ny,)), dma((ny,)),
            dma((ny,)), dma((nx,)),
        ],
        compiler_params=pltpu.CompilerParams(
            collective_id=0, has_side_effects=True, vmem_limit_bytes=60 * 1024 * 1024
        ),
    )(
        queries.reshape(rows, width), out_grad.reshape(rows, width), keys, values, limits,
        block_start,
    )
    dq, dk, dv = pl.pallas_call(
        place,
        out_shape=(
            jax.ShapeDtypeStruct((rows, width), f32),
            jax.ShapeDtypeStruct(keys.shape, f32),
            jax.ShapeDtypeStruct(values.shape, f32),
        ),
        in_specs=[in_vmem] * 2,
        out_specs=[in_hbm] * 3,
        scratch_shapes=[
            vmem((rows, width), f32), vmem(keys.shape, f32), vmem(values.shape, f32), dma((3,)),
        ],
    )(out_in, dq_in)
    return dq[None], dk, dv


def solution(mesh):
    ny = mesh.shape["seq"] // 2
    nx = ny
    nz = mesh.shape["frame"] // nx
    wide = P("frame", "seq", None)
    return jax.shard_map(
        functools.partial(body, nx, ny, nz),
        mesh=mesh,
        in_specs=(wide, wide, wide, wide, P("seq"), P("frame")),
        out_specs=(wide, wide, wide),
        check_vma=False,
    )
```

time: 1120 us -> 47.8 us (0.04)
  waiting for transfers between devices: 636 us -> 0 us
  matrix products: 159 us -> 0 us
  blocking collectives: 120 us -> 0 us
  loops' own time: 95.6 us -> 0 us
  local copies, waits for them, and re-layouts: 51.1 us -> 0 us
  Pallas kernels: 0 us -> 46.4 us
  other arithmetic: 32.4 us -> 0 us
  between operations: 14.6 us -> 1.29 us
    all_gather x6 -> x0, waiting for transfers between devices: 334 us -> none  [the longest x2 148 us: merged(): everything = jax.tree.map(lambda part: lax.all_gather(part, axis), shard)]
    reduce_scatter x3 -> x0, waiting for transfers between devices: 300 us -> none  [the longest x1 222 us: body(): lax.psum_scatter(dq_terms, 'frame', scatter_dimension=0, tiled=True)]
    dot_general x128 -> x0, matrix products: 159 us -> none  [the longest x48 57 us: scores_of(): jnp.einsum('hrd,fhd->hrf', q_part, k_part, preferred_element_type=jnp.flo...]
    psum x1 -> x0, blocking collectives: 120 us -> none  [body(): delta = lax.psum(local_delta, 'frame')]
    another operation x7 -> x0, loops' own time: 95.6 us -> none  [the longest x2 31.7 us: accumulate(): state, dq_groups = lax.scan(step, carry, starts)]
    pallas_call x0 -> x2, Pallas kernels: none -> 46.4 us  [the longest x1 44.3 us: body(): pl.pallas_call(functools.partial(kernel, nx, ny, nz), out_shape=(jax.Shap...]
    dynamic_slice x48 -> x0, local copies, waits for them, and re-layouts: 28.1 us -> none  [stats_block(): top_here, total_here = lax.map(stats_one_group, starts)]
    add x32 -> x0, other arithmetic: 25.3 us -> none  [the longest x31 25.3 us: combine(): first[1] * jnp.exp(first[0] - top) + second[1] * jnp.exp(second[0] - top)]
  transfers between devices with their start and end apart: 9 -> 0, of which waited for: 9 -> 0; matrix products, arithmetic and copies ran while one was open for 4% -> 0% of each run, Pallas kernels for 0% -> 0%
where the time goes in v1:
time: 47.8 us; the launch traced here: 47.7 us
  Pallas kernels  46.4 us (97%)
  between operations  1.29 us (3%)
    pallas_call x1, Pallas kernels, body(): pl.pallas_call(functools.partial(kernel, nx, ny, nz), out_shape=(jax.Shap...  44.3 us
    pallas_call x1, Pallas kernels, body(): pl.pallas_call(place, out_shape=(jax.ShapeDtypeStruct((rows, width), f32)...  2.16 us

profile of v1, /device:TPU:4, one launch (start us, length us, event | category | flops | bytes accessed | tf_op | source)
XLA Modules:
  0.0 47.7 jit_solution(9633242484809370499)
XLA Ops:
  1.3 44.3 %shard_map.85 = (bf16[4,2,128,128]{3,2,1,0:T(8,128)(2,1)}, f32[4,256,128]{2,1,0:T(8,128)}) custom-call(bf16[256,128]{1,0:T(8,128)(2,1)} %bitcast.4, bf16[256,128]{1,0:T(8,128)(2,1)} %bitcast.5, bf16[128,4,128]{2,1,0:T(4,128)(2,1)} %k_hbm.1, bf16[128,4,128]{2,1,0:T(4,128)(2,1)} %v_hbm.1, s32[2,128]{1,0:T(2,128)} %bitcast.6, s32[1]{0:T(128)S(6)} %copy.9.bs_ref), custom_call_target="tpu_custom_call" | custom-call | tf_op jit(solution)/shard_map/pallas_call | solution.py:381
  45.6 2.2 %shard_map.86 = (f32[256,128]{1,0:T(8,128)}, f32[128,4,128]{2,1,0:T(4,128)}, f32[128,4,128]{2,1,0:T(4,128)}) custom-call(bf16[4,2,128,128]{3,2,1,0:T(8,128)(2,1)} %get-tuple-element.8.out_in, f32[4,256,128]{2,1,0:T(8,128)} %get-tuple-element.9.dq_in), custom_call_target="tpu_custom_call" | custom-call | tf_op jit(solution)/shard_map/pallas_call | solution.py:428

commit v2 on v1

--- a/solution.py
+++ b/solution.py
@@ -11,6 +11,7 @@
 NEG = -1e30
 FLOOR = -1e29
 NT = (((1,), (1,)), ((), ()))
+TN = (((0,), (0,)), ((), ()))
 
 
 def kernel(
@@ -104,6 +105,7 @@
     for j in range(heads):
         stage[j, 2 * frames :] = start_rows.astype(jnp.bfloat16)
     part[...] = jnp.zeros_like(part)
+    kt[:, width:] = jnp.ones_like(kt[:, width:])
     fetches[0].wait()
     for j in range(heads):
         stage[j, 0:frames] = k_ref[:, j, :]
@@ -196,11 +198,11 @@
     def take(b):
         arrived(kv_all.at[b], kv_rs.at[b])
         remote(kv_all.at[b], kv_all.at[b], fw_ss.at[b], kv_rs.at[b], partner).start()
-        kt[b] = kv_all[b, 0:frames].T
+        kt[b, 0:width] = kv_all[b, 0:frames].T
 
     def take_passed(b):
         arrived(kv_all.at[b], kv_rs.at[b])
-        kt[b] = kv_all[b, 0:frames].T
+        kt[b, 0:width] = kv_all[b, 0:frames].T
 
     def first_step(n, _):
         b, b2 = pair(n)
@@ -218,7 +220,7 @@
 
     def near_blocks(i):
         text_arrived(i)
-        lax.fori_loop(0, heads - 1, functools.partial(step, i), 0)
+        lax.fori_loop(0, heads - 1, functools.partial(step, i), 0, unroll=True)
 
     def far_blocks(k, _):
         i = near(k)
@@ -237,7 +239,7 @@
     lax.fori_loop(0, max(ny - 1, 2), far_blocks, 0)
     if ny > 2:
         text_arrived(near(ny - 1))
-        lax.fori_loop(0, heads, functools.partial(step, near(ny - 1)), 0)
+        lax.fori_loop(0, heads, functools.partial(step, near(ny - 1)), 0, unroll=True)
         share_stats(near(ny - 1))
 
     def part_msg(t):
@@ -264,7 +266,27 @@
     def far(t):
         return lax.rem(zt + [2, 1, 3, 0][t] if heads == 4 else zt + t, heads)
 
-    def grads_chunk(i, last):
+    mean = sum(
+        jnp.sum(kv_all[b, 0:frames].astype(jnp.float32), axis=0, keepdims=True) for b in range(nz)
+    ) * (1.0 / (nz * frames))
+    mean = mean.astype(jnp.bfloat16).astype(jnp.float32)
+    mean_col = jnp.broadcast_to(mean, (width, width)).T
+    spot = lax.broadcasted_iota(jnp.int32, (16, width), 0)
+
+    def pack_dq(dst, terms):
+        extra = jnp.where(spot == 3 * (rows // width), mean, 0.0)
+        for n in range(rows // width):
+            cols = slice(n * width, (n + 1) * width)
+            whole = terms[width : width + 1, cols]
+            dst[cols] = ((terms[0:width, cols] - mean_col * whole).T * factor).astype(jnp.bfloat16)
+            rest = whole * factor
+            for m in range(3):
+                piece = rest.astype(jnp.bfloat16).astype(jnp.float32)
+                extra = jnp.where(spot == 3 * n + m, piece, extra)
+                rest = rest - piece
+        dst[rows:] = extra.astype(jnp.bfloat16)
+
+    def grads_chunk(i, last, dst):
         for n in range(nx):
             @pl.when(jnp.logical_not(x_self[n]))
             def _(n=n):
@@ -275,7 +297,7 @@
         shares = [jnp.exp(s[0:1] - top) for s in stats]
         total = sum(w * s[1:2] for w, s in zip(shares, stats))
         delta = sum(w * s[2:3] for w, s in zip(shares, stats)) / total
-        dqt = jnp.zeros((width, rows), jnp.float32)
+        dqt = jnp.zeros((width + 16, rows), jnp.float32)
         for n in range(heads):
             t = far(n)
             ds, low = [], []
@@ -295,20 +317,20 @@
                 jnp.concatenate(ds, axis=0),
                 preferred_element_type=jnp.float32,
             )
-        return dqt.T * factor
-
-    relay[y] = grads_chunk(y, False)
+        pack_dq(dst, dqt)
+
+    grads_chunk(y, False, relay.at[y])
     send(*dx_msg(y))
 
     def middle(k, _):
         i = near(k)
-        dq_send[i] = grads_chunk(i, False)
+        grads_chunk(i, False, dq_send.at[i])
         remote(*dy_msg(i)).start()
         return 0
 
     lax.fori_loop(1, ny - 1, middle, 0)
     i = near(ny - 1)
-    dq_send[i] = grads_chunk(i, True)
+    grads_chunk(i, True, dq_send.at[i])
     remote(*dy_msg(i)).start()
 
     def pass_on(a):
@@ -357,7 +379,21 @@
 
 
 def place(out_in, dq_in, dq_hbm, dk_hbm, dv_hbm, dq, dk, dv, sems):
-    dq[...] = functools.reduce(jnp.add, [dq_in[i] for i in range(dq_in.shape[0])])
+    rows, width = dq.shape
+    halves = rows // width
+    parts = range(dq_in.shape[0])
+    extra = [dq_in[i, rows:].astype(jnp.float32) for i in parts]
+    means = [jnp.broadcast_to(e[3 * halves : 3 * halves + 1], e.shape) for e in extra]
+    means = jnp.concatenate(means, axis=0).astype(jnp.bfloat16)
+    spot = lax.broadcasted_iota(jnp.int32, extra[0].shape, 0)
+    for n in range(halves):
+        here = slice(n * width, (n + 1) * width)
+        sums = [jnp.where(lax.div(spot, 3) == n, e, 0.0) for e in extra]
+        sums = jnp.concatenate(sums, axis=0).astype(jnp.bfloat16)
+        common = lax.dot_general(sums, means, TN, preferred_element_type=jnp.float32)
+        dq[here] = functools.reduce(
+            jnp.add, [dq_in[i, here].astype(jnp.float32) for i in parts], common
+        )
     writes = [pltpu.make_async_copy(dq, dq_hbm, sems.at[0])]
     writes[0].start()
     for n, (buf, hbm) in enumerate([(dk, dk_hbm), (dv, dv_hbm)]):
@@ -382,7 +418,7 @@
         functools.partial(kernel, nx, ny, nz),
         out_shape=(
             jax.ShapeDtypeStruct((heads, 2, frames, width), bf16),
-            jax.ShapeDtypeStruct((nx, rows, width), f32),
+            jax.ShapeDtypeStruct((nx, rows + 16, width), bf16),
         ),
         in_specs=[in_hbm] * 5 + [pl.BlockSpec(memory_space=pltpu.SMEM)],
         out_specs=[in_vmem] * 2,
@@ -394,7 +430,7 @@
             vmem(limits.shape, jnp.int32),
             vmem((heads, 2 * frames + 16, width), bf16),
             vmem((nz, 2 * frames + 16, width), bf16),
-            vmem((nz, width, frames), bf16),
+            vmem((nz, width + 16, frames), bf16),
             vmem((ny, rows, width), bf16),
             vmem((ny, rows, width), bf16),
             vmem((ny,) + limits.shape, jnp.int32),
@@ -407,8 +443,8 @@
             vmem((heads, 2, 2, frames, width), f32),
             vmem((heads, 2, frames, width), f32),
             vmem((heads, 2, frames, width), bf16),
-            vmem((ny, rows, width), f32),
-            vmem((ny, rows, width), f32),
+            vmem((ny, rows + 16, width), bf16),
+            vmem((ny, rows + 16, width), bf16),
             dma((5,)),
             dma((heads,)), dma((nz,)), dma((nz,)),
             dma((3, nx)), dma((3, ny)),

time: 47.8 us -> 44.1 us (0.923)
  the two profiles are of different devices: /device:TPU:4 before, /device:TPU:1 now
where the time goes in v2:
time: 44.1 us; the launch traced here: 44 us
  Pallas kernels  42.7 us (97%)
  between operations  1.29 us (3%)
    pallas_call x1, Pallas kernels, body(): pl.pallas_call(functools.partial(kernel, nx, ny, nz), out_shape=(jax.Shap...  40.5 us
    pallas_call x1, Pallas kernels, body(): pl.pallas_call(place, out_shape=(jax.ShapeDtypeStruct((rows, width), f32)...  2.2 us

profile of v2, /device:TPU:1, one launch (start us, length us, event | category | flops | bytes accessed | tf_op | source)
XLA Modules:
  0.0 44.0 jit_solution(15012332329029823406)
XLA Ops:
  1.3 40.5 %shard_map.85 = (bf16[4,2,128,128]{3,2,1,0:T(8,128)(2,1)}, bf16[4,272,128]{2,1,0:T(8,128)(2,1)}) custom-call(bf16[256,128]{1,0:T(8,128)(2,1)} %bitcast.4, bf16[256,128]{1,0:T(8,128)(2,1)} %bitcast.5, bf16[128,4,128]{2,1,0:T(4,128)(2,1)} %k_hbm.1, bf16[128,4,128]{2,1,0:T(4,128)(2,1)} %v_hbm.1, s32[2,128]{1,0:T(2,128)} %bitcast.6, s32[1]{0:T(128)S(6)} %copy.9.bs_ref), custom_call_target="tpu_custom_call" | custom-call | tf_op jit(solution)/shard_map/pallas_call | solution.py:417
  41.8 2.2 %shard_map.86 = (f32[256,128]{1,0:T(8,128)}, f32[128,4,128]{2,1,0:T(4,128)}, f32[128,4,128]{2,1,0:T(4,128)}) custom-call(bf16[4,2,128,128]{3,2,1,0:T(8,128)(2,1)} %get-tuple-element.8.out_in, bf16[4,272,128]{2,1,0:T(8,128)(2,1)} %get-tuple-element.9.dq_in), custom_call_target="tpu_custom_call" | custom-call | tf_op jit(solution)/shard_map/pallas_call | solution.py:464
